TPU v7x, 512 devices: a whole 4x8x8 slice. The times are simulated.
512 devices in a mesh: section: 16 (over y, core), tp: 32 (over z, x).
Axes of the slice: x: 4, y: 8, z: 8, core: 2. Of those that a mesh axis runs over, the one named last changes fastest.
Arguments:
- hidden: bfloat16 [16, 2, 256, 8192], P('section', None, None, 'tp'), may hold values from -400 to 400
- gain: float32 [16, 8192], P('section', 'tp'), may hold values from 0.5 to 1.5
- key_grad: bfloat16 [16, 2, 256, 1024], P('section', None, 'tp'), may hold values from -24 to 24
- master: float32 [16, 8192, 1024], P('section', 'tp'), may hold values from -0.0625 to 0.0625
- moment: float32 [16, 8192, 1024], P('section', 'tp'), may hold values from -0.00048828125 to 0.00048828125
- second: float32 [16, 8192, 1024], P('section', 'tp'), may hold values from 2.2351742e-11 to 2.23517418e-10
- overflow: int32 [16], P('section'), may hold values from 0 to 2
Outputs:
- grad_input: bfloat16 [16, 2, 256, 8192], P('section', None, None, 'tp')
- step: float32 [16, 8192, 1024], P('section', 'tp')
All inputs are finite; a program needn't handle non-finite values.
Results may differ from a plain program's by a relative error of at most 0.0049.
Values may be sent and summed in bfloat16 or wider, within the bound.
No kernel may reach another device: no remote copies, remote signals or barrier semaphores. Data moves between devices by JAX's collectives and lax.ppermute only.
A program may use at most 64 MiB of HBM per device.

v0:
```python
import jax
import jax.numpy as jnp
from jax import lax
from jax.experimental import pallas as pl
from jax.experimental.pallas import tpu as pltpu
from jax.sharding import Mesh, PartitionSpec as P

D = 8192
SEC, NZ, NX = 16, 8, 4
TP = NZ * NX
TOK = 512
F = 256
K = 1024
f32, bf16 = jnp.float32, jnp.bfloat16

beta_one = 0.9
beta_two = 0.999
decay = 0.1
clip_norm = 1.0
step_count = 10

VM = pl.BlockSpec(memory_space=pltpu.VMEM)
SM = pl.BlockSpec(memory_space=pltpu.SMEM)


def call(body, out_shape, n_in, flops=0, data=0, scratch=(), scalars=0):
    outs = (VM,) * len(out_shape) if isinstance(out_shape, tuple) else VM
    return pl.pallas_call(
        body,
        out_shape=out_shape,
        in_specs=[SM] * scalars + [VM] * n_in,
        out_specs=outs,
        scratch_shapes=list(scratch),
        compiler_params=pltpu.CompilerParams(vmem_limit_bytes=32 * 1024 * 1024),
        cost_estimate=pl.CostEstimate(flops=flops, bytes_accessed=data, transcendentals=0),
    )


def sds(shape, dtype=f32):
    return jax.ShapeDtypeStruct(shape, dtype)


RING = [3 * r % 8 for r in range(8)]
Y_PEERS = [y * 2 + core for core in range(2) for y in RING]


def swap(blocks, axis, peers=None):
    groups = None if peers is None else [peers]
    return lax.all_to_all(blocks, axis, split_axis=0, concat_axis=0, tiled=True, axis_index_groups=groups)


def split_rows(row):
    rows = jnp.concatenate([row[:, i * 128 : (i + 1) * 128] for i in range(4)], axis=0)
    high = rows.astype(bf16).astype(f32)
    low = rows - high
    return jnp.concatenate([high, low, jnp.zeros((8, 128), f32)], axis=0).astype(bf16)


def join_rows(rows):
    rows = rows.astype(f32)
    return rows[0:4] + rows[4:8]


def as_row(rows):
    return jnp.concatenate([rows[i : i + 1] for i in range(4)], axis=1)


def features_first(x_ref):
    x = x_ref[...].astype(f32).reshape(2, TP, 8, F)
    return jnp.concatenate([x[0][:, None], x[1][:, None]], axis=1).reshape(TOK, F).T


def first_kernel(x_ref, key_ref, send_ref):
    xt = features_first(x_ref)
    sums = split_rows(jnp.sum(xt * xt, axis=0, keepdims=True))
    for peer in range(NZ):
        for c in range(8):
            send_ref[peer, c * 16 : (c + 1) * 16, :] = key_ref[:, c * 128 : (c + 1) * 128]
        send_ref[peer, 128:136, :] = sums[0:8]


def middle_kernel(got_ref, send_ref):
    total = jnp.zeros((4, 128), f32)
    for z in range(NZ):
        total = total + join_rows(got_ref[z, 128:136, :])
    sums = split_rows(as_row(total))
    for peer in range(NX):
        for r, z in enumerate(RING):
            send_ref[peer, z * 128 : (z + 1) * 128, :] = got_ref[r, 0:128, :]
        send_ref[peer, 1024:1032, :] = sums[0:8]


def main_kernel(
    factor_ref, x_ref, got_ref, gain_ref, master_ref, gw_ref, plain_ref, slope_ref, send_ref, rows_ref, gx_ref
):
    for x in range(NX):
        for z in range(NZ):
            slot = z * NX + x
            for c in range(8):
                rows_ref[slot * 16 : (slot + 1) * 16, c * 128 : (c + 1) * 128] = got_ref[
                    x, z * 128 + c * 16 : z * 128 + (c + 1) * 16, :
                ]
    total = jnp.zeros((4, 128), f32)
    for x in range(NX):
        total = total + join_rows(got_ref[x, 1024:1032, :])
    inv = lax.rsqrt(as_row(total) * (1.0 / D) + 1e-05)
    col = jnp.broadcast_to(gain_ref[...], (8, F)).T[:, 0:1]
    xt = features_first(x_ref)
    gx = xt * col
    gx_ref[...] = (gx * inv).astype(bf16)
    slope_ref[...] = xt * (inv * inv * inv * (1.0 / D))
    factor = factor_ref[0]
    square = jnp.zeros((1, 256), f32)
    for n in range(4):
        cols = slice(n * 256, (n + 1) * 256)
        part = factor * jnp.dot(gx_ref[...], rows_ref[:, cols], preferred_element_type=f32)
        gw_ref[:, cols] = part
        square = square + jnp.sum(part * part, axis=0, keepdims=True)
    own_sq = jnp.broadcast_to(jnp.sum(square, axis=1, keepdims=True), (1, 128))
    weight = master_ref[...].astype(bf16)
    parts = []
    for n in range(2):
        cols = slice(n * 256, (n + 1) * 256)
        gh = lax.dot_general(
            weight, rows_ref[cols, :], (((1,), (1,)), ((), ())), preferred_element_type=f32
        )
        plain_ref[:, cols] = inv[:, cols] * (col * gh)
        parts.append(jnp.sum(gx[:, cols] * gh, axis=0, keepdims=True))
    packed = jnp.concatenate(parts + [own_sq], axis=1)
    for peer in range(TP):
        send_ref[peer] = packed


def branch_kernel(plain_ref, slope_ref, got_ref, send_ref):
    packed = got_ref[0]
    for peer in range(1, TP):
        packed = packed + got_ref[peer]
    sent = (plain_ref[...] - slope_ref[...] * packed[:, 0:TOK]).astype(bf16)
    layer_sq = split_rows(jnp.concatenate([packed[:, TOK:]] * 4, axis=1))
    for j in range(SEC):
        for q in range(4):
            send_ref[j, q * 16 : (q + 1) * 16, :] = sent[j * 16 : (j + 1) * 16, q * 128 : (q + 1) * 128]
        send_ref[j, 64:72, :] = layer_sq[0:8]


def suffix_kernel(got_ref, back_ref, clip_ref):
    running = jnp.zeros((64, 128), f32)
    norm = jnp.zeros((4, 128), f32)
    for layer in range(SEC - 1, -1, -1):
        s = Y_PEERS.index(layer)
        running = running + got_ref[s, 0:64, :].astype(f32)
        back_ref[s] = running.astype(bf16)
        norm = norm + join_rows(got_ref[s, 64:72, :])
    clip = jnp.minimum(1.0, clip_norm / (jnp.sqrt(norm) + 1e-06))
    clip_ref[...] = jnp.concatenate([clip, clip], axis=0)


def last_kernel(back_ref, out_ref):
    rows = []
    for j in range(SEC):
        rows.append(jnp.concatenate([back_ref[j, q * 16 : (q + 1) * 16, :] for q in range(4)], axis=1))
    out = jnp.concatenate(rows, axis=0).astype(f32).T.reshape(TP, 2, 8, F)
    for m in range(2):
        out_ref[m] = out[:, m].reshape(256, F).astype(bf16)


def on_device(hidden, gain, key_grad, master, moment, second, overflow):
    flag = overflow[0]
    factor = jnp.where(flag == 0, 1.0, jnp.where(flag == 1, 0.5, 0.0)).astype(f32)
    keep = jnp.where(flag == 2, 0.0, 1.0).astype(f32)

    send = call(first_kernel, sds((NZ, 136, 128), bf16), 2, 3 * F * TOK, F * TOK * 2)(
        hidden[0], key_grad.reshape(16, K)
    )
    got = swap(send, "z", RING)
    send = call(middle_kernel, sds((NX, 1032, 128), bf16), 1, 0, 1024 * 1024)(got)
    got = swap(send, "x")
    gw, plain, slope, send = call(
        main_kernel,
        (sds((F, K)), sds((F, TOK)), sds((F, TOK)), sds((TP, 1, TOK + 128))),
        4,
        4 * F * TOK * K,
        4 * 1024 * 1024,
        [pltpu.VMEM((TOK, K), bf16), pltpu.VMEM((F, TOK), bf16)],
        1,
    )(factor[None], hidden[0], got, gain, master[0])
    got = swap(send, ("z", "x"))
    send = call(branch_kernel, sds((SEC, 72, 128), bf16), 3, 3 * F * TOK, 1024 * 1024)(plain, slope, got)
    got = swap(send, ("y", "core"), Y_PEERS)
    back, clip = call(
        suffix_kernel, (sds((SEC, 64, 128), bf16), sds((8, 128))), 1, 4 * F * TOK, 1024 * 1024
    )(got)
    back = swap(back, ("y", "core"), Y_PEERS)
    clipped = clip[0, 0] * gw
    moment_new = beta_one * moment[0] + (1.0 - beta_one) * clipped
    second_new = beta_two * second[0] + (1.0 - beta_two) * clipped * clipped
    bias_one = 1.0 - beta_one**step_count
    bias_two = 1.0 - beta_two**step_count
    update = moment_new / bias_one / (jnp.sqrt(second_new / bias_two) + 1e-08) + decay * master[0]
    grad_input = call(last_kernel, sds((2, 256, F), bf16), 1, F * TOK, 1024 * 1024)(back)
    return (grad_input[None], (keep * update)[None])


def solution(mesh):
    fine = Mesh(mesh.devices.reshape(8, 2, NZ, NX), ("y", "core", "z", "x"))
    sec, tp = ("y", "core"), ("z", "x")
    return jax.shard_map(
        on_device,
        mesh=fine,
        in_specs=(
            P(sec, None, None, tp),
            P(sec, tp),
            P(sec, None, tp, None),
            P(sec, tp, None),
            P(sec, tp, None),
            P(sec, tp, None),
            P(sec),
        ),
        out_specs=(P(sec, None, None, tp), P(sec, tp, None)),
        check_vma=False,
    )
```

profile of v0, /device:TPU:1, one launch (start us, length us, event | category | flops | bytes accessed | tf_op | source)
XLA Modules:
  0.0 93.3 jit_solution(10264589891065274078)
XLA Ops:
  0.6 0.0 copy-start.1
  0.6 0.9 %copy-done.1 = bf16[1,2,256,256]{3,2,1,0:T(8,128)(2,1)S(1)} copy-done((bf16[1,2,256,256]{3,2,1,0:T(8,128)(2,1)S(1)}, bf16[1,2,256,256]{3,2,1,0:T(8,128)(2,1)}, u32[]{:S(2)}) %copy-start.1) | copy-done | bytes 262168
  1.6 0.0 copy-start.3
  1.6 0.8 copy-done.3
  2.3 0.2 shard_map.86
  2.5 20.5 %all_to_all.25.got_ref = bf16[8,136,128]{2,1,0:T(8,128)(2,1)S(1)} all-to-all(bf16[8,136,128]{2,1,0:T(8,128)(2,1)S(1)} %shard_map.86), channel_id=1, replica_groups={{0,12,24,4,16,28,8,20},{1,13,25,5,17,29,9,21},{2,14,26,6,18,30,10,22},{..., dimensions={0} | all-to-all | bytes 557056 | tf_op jit(solution)/shard_map/all_to_all | solution.py:49
  23.1 1.1 %shard_map.87 = bf16[4,1032,128]{2,1,0:T(8,128)(2,1)} custom-call(bf16[8,136,128]{2,1,0:T(8,128)(2,1)S(1)} %all_to_all.25.got_ref), custom_call_target="tpu_custom_call" | custom-call | bytes 1048576 | tf_op jit(solution)/shard_map/pallas_call | solution.py:176
  24.2 4.1 %all-to-all-start.1 = ((bf16[4,1032,128]{2,1,0:T(8,128)(2,1)}), bf16[4,1032,128]{2,1,0:T(8,128)(2,1)S(1)}, u32[]{:S(2)}, u32[]{:S(2)}) async-start(bf16[4,1032,128]{2,1,0:T(8,128)(2,1)} %shard_map.87), calls=%async_computation.1 | async-start | bytes 2113536 | tf_op jit(solution)/shard_map/all_to_all | solution.py:49
  29.0 10.7 %all-to-all-done.1.got_ref = bf16[4,1032,128]{2,1,0:T(8,128)(2,1)S(1)} async-done(((bf16[4,1032,128]{2,1,0:T(8,128)(2,1)}), bf16[4,1032,128]{2,1,0:T(8,128)(2,1)S(1)}, u32[]{:S(2)}, u32[]{:S(2)}) %all-to-all-start.1) | async-done | bytes 1056800 | tf_op jit(solution)/shard_map/all_to_all | solution.py:49
  39.7 0.0 copy-done
  39.7 0.0 copy-done.2
  39.7 0.0 copy-done.4
  39.7 1.0 %shard_map.88 = (f32[256,1024]{1,0:T(8,128)S(1)}, f32[256,512]{1,0:T(8,128)S(1)}, f32[256,512]{1,0:T(8,128)S(1)}, f32[32,1,640]{2,1,0:T(1,128)S(1)}) custom-call(f32[1]{0:T(128)S(6)} %select_n.17.factor_ref, bf16[2,256,256]{2,1,0:T(8,128)(2,1)S(1)} %bitcast.23, bf16[4,1032,128]{2,1,0:T(8,128)(2,1)S(1)} %all-to-all-done.1.got_ref, f32[1,256]{1,0:T(1,128)S(1)} %copy-done.4, ...), custom_call_target="tpu_custom_call" | custom-call | flops 536870912 | bytes 4194304 | tf_op jit(solution)/shard_map/pallas_call | solution.py:178
  40.7 16.5 %all_to_all.26.got_ref = f32[32,1,640]{2,1,0:T(1,128)S(1)} all-to-all(f32[32,1,640]{2,1,0:T(1,128)S(1)} %get-tuple-element.10), channel_id=1, replica_groups=mesh['y'=8,'core'=2,'z'=8,'x'=4] {'z','x'}, dimensions={0} | all-to-all | bytes 163840 | tf_op jit(solution)/shard_map/all_to_all | solution.py:49
  57.2 0.1 shard_map.89
  57.3 0.0 copy-start.5
  57.3 19.8 %all_to_all.27.got_ref = bf16[16,72,128]{2,1,0:T(8,128)(2,1)S(1)} all-to-all(bf16[16,72,128]{2,1,0:T(8,128)(2,1)S(1)} %shard_map.89), channel_id=1, replica_groups={{0,192,384,64,256,448,128,320,32,224,416,96,288,480,160,352},{1,193,385..., dimensions={0} | all-to-all | bytes 589824 | tf_op jit(solution)/shard_map/all_to_all | solution.py:49
  77.2 0.7 shard_map.90
  77.9 6.0 %all-to-all-start.4 = ((bf16[16,64,128]{2,1,0:T(8,128)(2,1)}), bf16[16,64,128]{2,1,0:T(8,128)(2,1)S(1)}, u32[]{:S(2)}, u32[]{:S(2)}) async-start(bf16[16,64,128]{2,1,0:T(8,128)(2,1)} %get-tuple-element.11), calls=%async_computation.4 | async-start | bytes 524288 | tf_op jit(solution)/shard_map/all_to_all | solution.py:49
  83.9 0.6 slice.3
  84.4 0.0 copy-done.5
  84.4 3.6 %multiply_bitcast_fusion = f32[1,256,1024]{2,1,0:T(8,128)} fusion(f32[1,256,1024]{2,1,0:T(8,128)S(1)} %copy-done.5, f32[256,1024]{1,0:T(8,128)S(1)} %get-tuple-element.13, f32[1,256,1024]{2,1,0:T(8,128)} %param.11, f32[]{:T(128)} %bitcast.6, f32[]{:T(128)} %bitcast.4, f32[1,256,1024]{2,1,0:T(8,128)S(1)} %copy-done), kind=kLoop, calls=%fused_computation.9 | loop fusion | flops 3932160 | bytes 5242888 | tf_op jit(solution)/shard_map/broadcast_in_dim | solution.py:201
  88.0 4.5 %all-to-all-done.4.back_ref = bf16[16,64,128]{2,1,0:T(8,128)(2,1)S(1)} async-done(((bf16[16,64,128]{2,1,0:T(8,128)(2,1)}), bf16[16,64,128]{2,1,0:T(8,128)(2,1)S(1)}, u32[]{:S(2)}, u32[]{:S(2)}) %all-to-all-start.4) | async-done | bytes 262176 | tf_op jit(solution)/shard_map/all_to_all | solution.py:49
  92.5 0.8 shard_map.91
  (3 shorter events, 0.0 us)
Async XLA Ops:
  0.6 1.0 %copy-start.1 = (bf16[1,2,256,256]{3,2,1,0:T(8,128)(2,1)S(1)}, bf16[1,2,256,256]{3,2,1,0:T(8,128)(2,1)}, u32[]{:S(2)}) copy-start(bf16[1,2,256,256]{3,2,1,0:T(8,128)(2,1)} %param.7) | copy-start | bytes 786436
  1.6 0.8 copy-start.3
  24.2 15.5 %copy-start = (f32[1,256,1024]{2,1,0:T(8,128)S(1)}, f32[1,256,1024]{2,1,0:T(8,128)}, u32[]{:S(2)}) copy-start(f32[1,256,1024]{2,1,0:T(8,128)} %param.10) | copy-start | bytes 3145732
  24.2 15.5 %copy-start.2 = (bf16[1,2,256,256]{3,2,1,0:T(8,128)(2,1)S(1)}, bf16[1,2,256,256]{3,2,1,0:T(8,128)(2,1)}, u32[]{:S(2)}) copy-start(bf16[1,2,256,256]{3,2,1,0:T(8,128)(2,1)} %param.7) | copy-start | bytes 786436
  24.2 15.5 %copy-start.4 = (f32[1,256]{1,0:T(1,128)S(1)}, f32[1,256]{1,0:T(1,128)}, u32[]{:S(2)}) copy-start(f32[1,256]{1,0:T(1,128)} %gain_ref.1) | copy-start | bytes 3076
  24.2 15.5 %all-to-all-start.1 = ((bf16[4,1032,128]{2,1,0:T(8,128)(2,1)}), bf16[4,1032,128]{2,1,0:T(8,128)(2,1)S(1)}, u32[]{:S(2)}, u32[]{:S(2)}) async-start(bf16[4,1032,128]{2,1,0:T(8,128)(2,1)} %shard_map.87), calls=%async_computation.1 | async-start | bytes 2113536 | tf_op jit(solution)/shard_map/all_to_all | solution.py:49
  57.3 27.1 %copy-start.5 = (f32[1,256,1024]{2,1,0:T(8,128)S(1)}, f32[1,256,1024]{2,1,0:T(8,128)}, u32[]{:S(2)}) copy-start(f32[1,256,1024]{2,1,0:T(8,128)} %param.12) | copy-start | bytes 3145732
  77.9 14.6 %all-to-all-start.4 = ((bf16[16,64,128]{2,1,0:T(8,128)(2,1)}), bf16[16,64,128]{2,1,0:T(8,128)(2,1)S(1)}, u32[]{:S(2)}, u32[]{:S(2)}) async-start(bf16[16,64,128]{2,1,0:T(8,128)(2,1)} %get-tuple-element.11), calls=%async_computation.4 | async-start | bytes 524288 | tf_op jit(solution)/shard_map/all_to_all | solution.py:49
where the time goes:
time: 95.2 us; the launch traced here: 93.3 us
  blocking collectives  56.9 us (60%)
  waiting for transfers between devices  15.2 us (16%)
  starting transfers between devices  10.1 us (11%)
  Pallas kernels  3.94 us (4%)
  other arithmetic  3.61 us (4%)
  local copies, waits for them, and re-layouts  2.29 us (2%)
  between operations  1.33 us (1%)
    all_to_all x3, blocking collectives, swap(): lax.all_to_all(blocks, axis, split_axis=0, concat_axis=0, tiled=True, axi...  56.9 us
    all_to_all x2, waiting for transfers between devices, swap(): lax.all_to_all(blocks, axis, split_axis=0, concat_axis=0, tiled=True, axi...  15.2 us
    all_to_all x2, starting transfers between devices, swap(): lax.all_to_all(blocks, axis, split_axis=0, concat_axis=0, tiled=True, axi...  10.1 us
    broadcast_in_dim x1, other arithmetic, on_device(): return (grad_input[None], (keep * update)[None])  3.61 us
  transfers between devices with their start and end apart: 2, of which 2 were waited for; matrix products, arithmetic and copies ran while one was open for 4% of the time, Pallas kernels for 0%

commit v1 on v0

--- a/solution.py
+++ b/solution.py
@@ -70,13 +70,21 @@
     return jnp.concatenate([x[0][:, None], x[1][:, None]], axis=1).reshape(TOK, F).T
 
 
-def first_kernel(x_ref, key_ref, send_ref):
+def key_kernel(key_ref, block_ref):
+    for c in range(8):
+        block_ref[c * 16 : (c + 1) * 16, :] = key_ref[:, c * 128 : (c + 1) * 128]
+
+
+def first_kernel(flag_ref, x_ref, block_ref, send_ref, flags_ref):
     xt = features_first(x_ref)
     sums = split_rows(jnp.sum(xt * xt, axis=0, keepdims=True))
     for peer in range(NZ):
-        for c in range(8):
-            send_ref[peer, c * 16 : (c + 1) * 16, :] = key_ref[:, c * 128 : (c + 1) * 128]
+        send_ref[peer, 0:128, :] = block_ref[...]
         send_ref[peer, 128:136, :] = sums[0:8]
+    flag = flag_ref[0]
+    factor = jnp.where(flag == 0, 1.0, jnp.where(flag == 1, 0.5, 0.0)).astype(f32)
+    keep = jnp.where(flag == 2, 0.0, 1.0).astype(f32)
+    flags_ref[...] = jnp.concatenate([jnp.full((4, 128), factor), jnp.full((4, 128), keep)], axis=0)
 
 
 def middle_kernel(got_ref, send_ref):
@@ -91,7 +99,7 @@
 
 
 def main_kernel(
-    factor_ref, x_ref, got_ref, gain_ref, master_ref, gw_ref, plain_ref, slope_ref, send_ref, rows_ref, gx_ref
+    flags_ref, x_ref, got_ref, gain_ref, master_ref, gw_ref, plain_ref, slope_ref, send_ref, rows_ref, gx_ref
 ):
     for x in range(NX):
         for z in range(NZ):
@@ -109,7 +117,7 @@
     gx = xt * col
     gx_ref[...] = (gx * inv).astype(bf16)
     slope_ref[...] = xt * (inv * inv * inv * (1.0 / D))
-    factor = factor_ref[0]
+    factor = flags_ref[0:1, 0:1]
     square = jnp.zeros((1, 256), f32)
     for n in range(4):
         cols = slice(n * 256, (n + 1) * 256)
@@ -143,7 +151,7 @@
         send_ref[j, 64:72, :] = layer_sq[0:8]
 
 
-def suffix_kernel(got_ref, back_ref, clip_ref):
+def suffix_kernel(got_ref, flags_ref, back_ref, clip_ref):
     running = jnp.zeros((64, 128), f32)
     norm = jnp.zeros((4, 128), f32)
     for layer in range(SEC - 1, -1, -1):
@@ -152,7 +160,7 @@
         back_ref[s] = running.astype(bf16)
         norm = norm + join_rows(got_ref[s, 64:72, :])
     clip = jnp.minimum(1.0, clip_norm / (jnp.sqrt(norm) + 1e-06))
-    clip_ref[...] = jnp.concatenate([clip, clip], axis=0)
+    clip_ref[...] = jnp.concatenate([clip, flags_ref[4:8, :]], axis=0)
 
 
 def last_kernel(back_ref, out_ref):
@@ -165,31 +173,27 @@
 
 
 def on_device(hidden, gain, key_grad, master, moment, second, overflow):
-    flag = overflow[0]
-    factor = jnp.where(flag == 0, 1.0, jnp.where(flag == 1, 0.5, 0.0)).astype(f32)
-    keep = jnp.where(flag == 2, 0.0, 1.0).astype(f32)
-
-    send = call(first_kernel, sds((NZ, 136, 128), bf16), 2, 3 * F * TOK, F * TOK * 2)(
-        hidden[0], key_grad.reshape(16, K)
-    )
+    block = call(key_kernel, sds((128, 128), bf16), 1, 0, 64 * 1024)(key_grad.reshape(16, K))
+    send, flags = call(
+        first_kernel, (sds((NZ, 136, 128), bf16), sds((8, 128))), 2, 3 * F * TOK, F * TOK * 2, (), 1
+    )(overflow, hidden[0], block)
     got = swap(send, "z", RING)
     send = call(middle_kernel, sds((NX, 1032, 128), bf16), 1, 0, 1024 * 1024)(got)
     got = swap(send, "x")
     gw, plain, slope, send = call(
         main_kernel,
         (sds((F, K)), sds((F, TOK)), sds((F, TOK)), sds((TP, 1, TOK + 128))),
-        4,
+        5,
         4 * F * TOK * K,
         4 * 1024 * 1024,
         [pltpu.VMEM((TOK, K), bf16), pltpu.VMEM((F, TOK), bf16)],
-        1,
-    )(factor[None], hidden[0], got, gain, master[0])
+    )(flags, hidden[0], got, gain, master[0])
     got = swap(send, ("z", "x"))
     send = call(branch_kernel, sds((SEC, 72, 128), bf16), 3, 3 * F * TOK, 1024 * 1024)(plain, slope, got)
     got = swap(send, ("y", "core"), Y_PEERS)
     back, clip = call(
-        suffix_kernel, (sds((SEC, 64, 128), bf16), sds((8, 128))), 1, 4 * F * TOK, 1024 * 1024
-    )(got)
+        suffix_kernel, (sds((SEC, 64, 128), bf16), sds((8, 128))), 2, 4 * F * TOK, 1024 * 1024
+    )(got, flags)
     back = swap(back, ("y", "core"), Y_PEERS)
     clipped = clip[0, 0] * gw
     moment_new = beta_one * moment[0] + (1.0 - beta_one) * clipped
@@ -198,7 +202,7 @@
     bias_two = 1.0 - beta_two**step_count
     update = moment_new / bias_one / (jnp.sqrt(second_new / bias_two) + 1e-08) + decay * master[0]
     grad_input = call(last_kernel, sds((2, 256, F), bf16), 1, F * TOK, 1024 * 1024)(back)
-    return (grad_input[None], (keep * update)[None])
+    return (grad_input[None], (clip[4, 0] * update)[None])
 
 
 def solution(mesh):

time: 95.2 us -> 94.7 us (level)
  blocking collectives: 56.9 us -> 72.2 us
  waiting for transfers between devices: 15.2 us -> 3.79 us
  starting transfers between devices: 10.1 us -> 5.95 us
  Pallas kernels: 3.94 us -> 2.97 us
    all_to_all x3 -> x4, blocking collectives: 56.9 us -> 72.2 us  [swap(): lax.all_to_all(blocks, axis, split_axis=0, concat_axis=0, tiled=True, axi...]
    all_to_all x2 -> x1, waiting for transfers between devices: 15.2 us -> 3.79 us  [swap(): lax.all_to_all(blocks, axis, split_axis=0, concat_axis=0, tiled=True, axi...]
    all_to_all x2 -> x1, starting transfers between devices: 10.1 us -> 5.95 us  [swap(): lax.all_to_all(blocks, axis, split_axis=0, concat_axis=0, tiled=True, axi...]
    pallas_call x1, Pallas kernels: 1.12 us -> 0.14 us  [on_device(): call(middle_kernel, sds((NX, 1032, 128), bf16), 1, 0, 1024 * 1024)(got)]
  transfers between devices with their start and end apart: 2 -> 1, of which waited for: 2 -> 1; matrix products, arithmetic and copies ran while one was open for 4% -> 5% of each run, Pallas kernels for 0% -> 0%
where the time goes in v1:
time: 94.7 us; the launch traced here: 92.8 us
  blocking collectives  72.2 us (76%)
  starting transfers between devices  5.95 us (6%)
  other arithmetic  4.26 us (4%)
  waiting for transfers between devices  3.79 us (4%)
  Pallas kernels  2.97 us (3%)
  local copies, waits for them, and re-layouts  2.3 us (2%)
  between operations  1.35 us (1%)
    all_to_all x4, blocking collectives, swap(): lax.all_to_all(blocks, axis, split_axis=0, concat_axis=0, tiled=True, axi...  72.2 us
    all_to_all x1, starting transfers between devices, swap(): lax.all_to_all(blocks, axis, split_axis=0, concat_axis=0, tiled=True, axi...  5.95 us
    broadcast_in_dim x1, other arithmetic, on_device(): return (grad_input[None], (clip[4, 0] * update)[None])  4.26 us
    all_to_all x1, waiting for transfers between devices, swap(): lax.all_to_all(blocks, axis, split_axis=0, concat_axis=0, tiled=True, axi...  3.79 us
  transfers between devices with their start and end apart: 1, of which 1 were waited for; matrix products, arithmetic and copies ran while one was open for 5% of the time, Pallas kernels for 0%

profile of v1, /device:TPU:1, one launch (start us, length us, event | category | flops | bytes accessed | tf_op | source)
XLA Modules:
  0.0 92.8 jit_solution(17320556904894057856)
XLA Ops:
  1.3 0.0 copy-start.3
  1.3 0.7 copy-done.3
  2.0 0.9 %copy-done.1 = bf16[1,2,256,256]{3,2,1,0:T(8,128)(2,1)S(1)} copy-done((bf16[1,2,256,256]{3,2,1,0:T(8,128)(2,1)S(1)}, bf16[1,2,256,256]{3,2,1,0:T(8,128)(2,1)}, u32[]{:S(2)}) %copy-start.1) | copy-done | bytes 262168
  3.0 0.2 shard_map.87
  3.2 20.5 %all_to_all.25.got_ref = bf16[8,136,128]{2,1,0:T(8,128)(2,1)S(1)} all-to-all(bf16[8,136,128]{2,1,0:T(8,128)(2,1)S(1)} %get-tuple-element.11), channel_id=1, replica_groups={{0,12,24,4,16,28,8,20},{1,13,25,5,17,29,9,21},{2,14,26,6,18,30,10,22},{..., dimensions={0} | all-to-all | bytes 557056 | tf_op jit(solution)/shard_map/all_to_all | solution.py:49
  23.7 0.1 shard_map.88
  23.8 0.0 copy-start
  23.9 0.0 copy-start.2
  23.9 0.0 copy-start.4
  23.9 15.3 %all_to_all.26.got_ref = bf16[4,1032,128]{2,1,0:T(8,128)(2,1)S(1)} all-to-all(bf16[4,1032,128]{2,1,0:T(8,128)(2,1)S(1)} %shard_map.88), channel_id=1, replica_groups=mesh['y'=8,'core'=2,'z'=8,'x'=4] {'x'}, dimensions={0} | all-to-all | bytes 2113536 | tf_op jit(solution)/shard_map/all_to_all | solution.py:49
  39.2 0.0 copy-done
  39.2 0.0 copy-done.2
  39.2 0.0 copy-done.4
  39.2 1.0 %shard_map.89 = (f32[256,1024]{1,0:T(8,128)S(1)}, f32[256,512]{1,0:T(8,128)S(1)}, f32[256,512]{1,0:T(8,128)S(1)}, f32[32,1,640]{2,1,0:T(1,128)S(1)}) custom-call(f32[8,128]{1,0:T(8,128)S(1)} %get-tuple-element.10.flags_ref, bf16[2,256,256]{2,1,0:T(8,128)(2,1)S(1)} %bitcast.23, bf16[4,1032,128]{2,1,0:T(8,128)(2,1)S(1)} %all_to_all.26.got_ref, ...), custom_call_target="tpu_custom_call" | custom-call | flops 536870912 | bytes 4194304 | tf_op jit(solution)/shard_map/pallas_call | solution.py:183
  40.2 16.6 %all_to_all.27.got_ref = f32[32,1,640]{2,1,0:T(1,128)S(1)} all-to-all(f32[32,1,640]{2,1,0:T(1,128)S(1)} %get-tuple-element.14), channel_id=1, replica_groups=mesh['y'=8,'core'=2,'z'=8,'x'=4] {'z','x'}, dimensions={0} | all-to-all | bytes 163840 | tf_op jit(solution)/shard_map/all_to_all | solution.py:49
  56.8 0.1 shard_map.90
  56.8 0.0 copy-start.5
  56.9 19.8 %all_to_all.28.got_ref = bf16[16,72,128]{2,1,0:T(8,128)(2,1)S(1)} all-to-all(bf16[16,72,128]{2,1,0:T(8,128)(2,1)S(1)} %shard_map.90), channel_id=1, replica_groups={{0,192,384,64,256,448,128,320,32,224,416,96,288,480,160,352},{1,193,385..., dimensions={0} | all-to-all | bytes 589824 | tf_op jit(solution)/shard_map/all_to_all | solution.py:49
  76.7 0.7 shard_map.91
  77.4 6.0 %all-to-all-start.4 = ((bf16[16,64,128]{2,1,0:T(8,128)(2,1)}), bf16[16,64,128]{2,1,0:T(8,128)(2,1)S(1)}, u32[]{:S(2)}, u32[]{:S(2)}) async-start(bf16[16,64,128]{2,1,0:T(8,128)(2,1)} %get-tuple-element.15), calls=%async_computation.4 | async-start | bytes 524288 | tf_op jit(solution)/shard_map/all_to_all | solution.py:49
  83.4 0.6 fusion.7
  84.0 4.3 %multiply_bitcast_fusion = f32[1,256,1024]{2,1,0:T(8,128)} fusion(f32[1,256,1024]{2,1,0:T(8,128)S(1)} %copy-done.5, f32[256,1024]{1,0:T(8,128)S(1)} %get-tuple-element.17, f32[1,256,1024]{2,1,0:T(8,128)} %param.11, f32[]{:T(128)} %bitcast.6, f32[]{:T(128)} %bitcast.4, f32[1,256,1024]{2,1,0:T(8,128)S(1)} %copy-done), kind=kLoop, calls=%fused_computation.9 | loop fusion | flops 3932160 | bytes 5242888 | tf_op jit(solution)/shard_map/broadcast_in_dim | solution.py:205
  88.2 3.8 %all-to-all-done.4.back_ref = bf16[16,64,128]{2,1,0:T(8,128)(2,1)S(1)} async-done(((bf16[16,64,128]{2,1,0:T(8,128)(2,1)}), bf16[16,64,128]{2,1,0:T(8,128)(2,1)S(1)}, u32[]{:S(2)}, u32[]{:S(2)}) %all-to-all-start.4) | async-done | bytes 262176 | tf_op jit(solution)/shard_map/all_to_all | solution.py:49
  92.0 0.8 shard_map.92
  (3 shorter events, 0.0 us)
Async XLA Ops:
  1.3 0.8 copy-start.3
  2.0 0.9 %copy-start.1 = (bf16[1,2,256,256]{3,2,1,0:T(8,128)(2,1)S(1)}, bf16[1,2,256,256]{3,2,1,0:T(8,128)(2,1)}, u32[]{:S(2)}) copy-start(bf16[1,2,256,256]{3,2,1,0:T(8,128)(2,1)} %param.7) | copy-start | bytes 786436
  23.8 15.4 %copy-start = (f32[1,256,1024]{2,1,0:T(8,128)S(1)}, f32[1,256,1024]{2,1,0:T(8,128)}, u32[]{:S(2)}) copy-start(f32[1,256,1024]{2,1,0:T(8,128)} %param.10) | copy-start | bytes 3145732
  23.9 15.4 %copy-start.2 = (bf16[1,2,256,256]{3,2,1,0:T(8,128)(2,1)S(1)}, bf16[1,2,256,256]{3,2,1,0:T(8,128)(2,1)}, u32[]{:S(2)}) copy-start(bf16[1,2,256,256]{3,2,1,0:T(8,128)(2,1)} %param.7) | copy-start | bytes 786436
  23.9 15.3 %copy-start.4 = (f32[1,256]{1,0:T(1,128)S(1)}, f32[1,256]{1,0:T(1,128)}, u32[]{:S(2)}) copy-start(f32[1,256]{1,0:T(1,128)} %gain_ref.1) | copy-start | bytes 3076
  56.8 27.1 %copy-start.5 = (f32[1,256,1024]{2,1,0:T(8,128)S(1)}, f32[1,256,1024]{2,1,0:T(8,128)}, u32[]{:S(2)}) copy-start(f32[1,256,1024]{2,1,0:T(8,128)} %param.12) | copy-start | bytes 3145732
  77.4 14.6 %all-to-all-start.4 = ((bf16[16,64,128]{2,1,0:T(8,128)(2,1)}), bf16[16,64,128]{2,1,0:T(8,128)(2,1)S(1)}, u32[]{:S(2)}, u32[]{:S(2)}) async-start(bf16[16,64,128]{2,1,0:T(8,128)(2,1)} %get-tuple-element.15), calls=%async_computation.4 | async-start | bytes 524288 | tf_op jit(solution)/shard_map/all_to_all | solution.py:49

commit v2 on v1

--- a/solution.py
+++ b/solution.py
@@ -40,7 +40,8 @@
     return jax.ShapeDtypeStruct(shape, dtype)
 
 
-RING = [3 * r % 8 for r in range(8)]
+RING = [0, 1, 7, 2, 6, 3, 5, 4]
+X_RING = [0, 1, 3, 2]
 Y_PEERS = [y * 2 + core for core in range(2) for y in RING]
 
 
@@ -101,12 +102,12 @@
 def main_kernel(
     flags_ref, x_ref, got_ref, gain_ref, master_ref, gw_ref, plain_ref, slope_ref, send_ref, rows_ref, gx_ref
 ):
-    for x in range(NX):
+    for r, x in enumerate(X_RING):
         for z in range(NZ):
             slot = z * NX + x
             for c in range(8):
                 rows_ref[slot * 16 : (slot + 1) * 16, c * 128 : (c + 1) * 128] = got_ref[
-                    x, z * 128 + c * 16 : z * 128 + (c + 1) * 16, :
+                    r, z * 128 + c * 16 : z * 128 + (c + 1) * 16, :
                 ]
     total = jnp.zeros((4, 128), f32)
     for x in range(NX):
@@ -179,7 +180,7 @@
     )(overflow, hidden[0], block)
     got = swap(send, "z", RING)
     send = call(middle_kernel, sds((NX, 1032, 128), bf16), 1, 0, 1024 * 1024)(got)
-    got = swap(send, "x")
+    got = swap(send, "x", X_RING)
     gw, plain, slope, send = call(
         main_kernel,
         (sds((F, K)), sds((F, TOK)), sds((F, TOK)), sds((TP, 1, TOK + 128))),

time: 94.7 us -> 94.7 us (level); the launches traced: 92.8 us -> 94.1 us
  waiting for transfers between devices: 3.79 us -> 5.42 us
  starting transfers between devices: 5.95 us -> 4.36 us
  blocking collectives: 72.2 us -> 73.5 us
    all_to_all x1, waiting for transfers between devices: 3.79 us -> 5.42 us  [swap(): lax.all_to_all(blocks, axis, split_axis=0, concat_axis=0, tiled=True, axi...]
    all_to_all x1, starting transfers between devices: 5.95 us -> 4.36 us  [swap(): lax.all_to_all(blocks, axis, split_axis=0, concat_axis=0, tiled=True, axi...]
    all_to_all x4, blocking collectives: 72.2 us -> 73.5 us  [swap(): lax.all_to_all(blocks, axis, split_axis=0, concat_axis=0, tiled=True, axi...]
where the time goes in v2:
time: 94.7 us; the launch traced here: 94.1 us
  blocking collectives  73.5 us (78%)
  waiting for transfers between devices  5.42 us (6%)
  starting transfers between devices  4.36 us (5%)
  other arithmetic  4.26 us (4%)
  Pallas kernels  2.98 us (3%)
  local copies, waits for them, and re-layouts  2.3 us (2%)
  between operations  1.35 us (1%)
    all_to_all x4, blocking collectives, swap(): lax.all_to_all(blocks, axis, split_axis=0, concat_axis=0, tiled=True, axi...  73.5 us
    all_to_all x1, waiting for transfers between devices, swap(): lax.all_to_all(blocks, axis, split_axis=0, concat_axis=0, tiled=True, axi...  5.42 us
    all_to_all x1, starting transfers between devices, swap(): lax.all_to_all(blocks, axis, split_axis=0, concat_axis=0, tiled=True, axi...  4.36 us
    broadcast_in_dim x1, other arithmetic, on_device(): return (grad_input[None], (clip[4, 0] * update)[None])  4.26 us
  transfers between devices with their start and end apart: 1, of which 1 were waited for; matrix products, arithmetic and copies ran while one was open for 5% of the time, Pallas kernels for 0%

profile of v2, /device:TPU:1, one launch (start us, length us, event | category | flops | bytes accessed | tf_op | source)
XLA Modules:
  0.0 94.1 jit_solution(7075504588991826279)
XLA Ops:
  1.3 0.0 copy-start.3
  1.3 0.7 copy-done.3
  2.0 0.9 %copy-done.1 = bf16[1,2,256,256]{3,2,1,0:T(8,128)(2,1)S(1)} copy-done((bf16[1,2,256,256]{3,2,1,0:T(8,128)(2,1)S(1)}, bf16[1,2,256,256]{3,2,1,0:T(8,128)(2,1)}, u32[]{:S(2)}) %copy-start.1) | copy-done | bytes 262168
  3.0 0.2 shard_map.87
  3.2 22.1 %all_to_all.25.got_ref = bf16[8,136,128]{2,1,0:T(8,128)(2,1)S(1)} all-to-all(bf16[8,136,128]{2,1,0:T(8,128)(2,1)S(1)} %get-tuple-element.11), channel_id=1, replica_groups={{0,4,28,8,24,12,20,16},{1,5,29,9,25,13,21,17},{2,6,30,10,26,14,22,18},{..., dimensions={0} | all-to-all | bytes 557056 | tf_op jit(solution)/shard_map/all_to_all | solution.py:50
  25.2 0.1 shard_map.88
  25.4 0.0 copy-start
  25.4 0.0 copy-start.2
  25.4 0.0 copy-start.4
  25.4 17.1 %all_to_all.26.got_ref = bf16[4,1032,128]{2,1,0:T(8,128)(2,1)S(1)} all-to-all(bf16[4,1032,128]{2,1,0:T(8,128)(2,1)S(1)} %shard_map.88), channel_id=1, replica_groups={{0,1,3,2},{4,5,7,6},{8,9,11,10},{12,13,15,14},{16,17,19,18},{20,21,23,2..., dimensions={0} | all-to-all | bytes 2113536 | tf_op jit(solution)/shard_map/all_to_all | solution.py:50
  42.5 0.0 copy-done
  42.5 0.0 copy-done.2
  42.5 0.0 copy-done.4
  42.5 1.0 %shard_map.89 = (f32[256,1024]{1,0:T(8,128)S(1)}, f32[256,512]{1,0:T(8,128)S(1)}, f32[256,512]{1,0:T(8,128)S(1)}, f32[32,1,640]{2,1,0:T(1,128)S(1)}) custom-call(f32[8,128]{1,0:T(8,128)S(1)} %get-tuple-element.10.flags_ref, bf16[2,256,256]{2,1,0:T(8,128)(2,1)S(1)} %bitcast.23, bf16[4,1032,128]{2,1,0:T(8,128)(2,1)S(1)} %all_to_all.26.got_ref, ...), custom_call_target="tpu_custom_call" | custom-call | flops 536870912 | bytes 4194304 | tf_op jit(solution)/shard_map/pallas_call | solution.py:184
  43.5 12.6 %all_to_all.27.got_ref = f32[32,1,640]{2,1,0:T(1,128)S(1)} all-to-all(f32[32,1,640]{2,1,0:T(1,128)S(1)} %get-tuple-element.14), channel_id=1, replica_groups=mesh['y'=8,'core'=2,'z'=8,'x'=4] {'z','x'}, dimensions={0} | all-to-all | bytes 163840 | tf_op jit(solution)/shard_map/all_to_all | solution.py:50
  56.1 0.1 shard_map.90
  56.2 0.0 copy-start.5
  56.2 21.7 %all_to_all.28.got_ref = bf16[16,72,128]{2,1,0:T(8,128)(2,1)S(1)} all-to-all(bf16[16,72,128]{2,1,0:T(8,128)(2,1)S(1)} %shard_map.90), channel_id=1, replica_groups={{0,64,448,128,384,192,320,256,32,96,480,160,416,224,352,288},{1,65,449,..., dimensions={0} | all-to-all | bytes 589824 | tf_op jit(solution)/shard_map/all_to_all | solution.py:50
  77.9 0.7 shard_map.91
  78.7 4.4 %all-to-all-start.4 = ((bf16[16,64,128]{2,1,0:T(8,128)(2,1)}), bf16[16,64,128]{2,1,0:T(8,128)(2,1)S(1)}, u32[]{:S(2)}, u32[]{:S(2)}) async-start(bf16[16,64,128]{2,1,0:T(8,128)(2,1)} %get-tuple-element.15), calls=%async_computation.4 | async-start | bytes 524288 | tf_op jit(solution)/shard_map/all_to_all | solution.py:50
  83.0 0.6 fusion.7
  83.6 4.3 %multiply_bitcast_fusion = f32[1,256,1024]{2,1,0:T(8,128)} fusion(f32[1,256,1024]{2,1,0:T(8,128)S(1)} %copy-done.5, f32[256,1024]{1,0:T(8,128)S(1)} %get-tuple-element.17, f32[1,256,1024]{2,1,0:T(8,128)} %param.11, f32[]{:T(128)} %bitcast.6, f32[]{:T(128)} %bitcast.4, f32[1,256,1024]{2,1,0:T(8,128)S(1)} %copy-done), kind=kLoop, calls=%fused_computation.9 | loop fusion | flops 3932160 | bytes 5242888 | tf_op jit(solution)/shard_map/broadcast_in_dim | solution.py:206
  87.9 5.4 %all-to-all-done.4.back_ref = bf16[16,64,128]{2,1,0:T(8,128)(2,1)S(1)} async-done(((bf16[16,64,128]{2,1,0:T(8,128)(2,1)}), bf16[16,64,128]{2,1,0:T(8,128)(2,1)S(1)}, u32[]{:S(2)}, u32[]{:S(2)}) %all-to-all-start.4) | async-done | bytes 262176 | tf_op jit(solution)/shard_map/all_to_all | solution.py:50
  93.3 0.8 shard_map.92
  (3 shorter events, 0.0 us)
Async XLA Ops:
  1.3 0.8 copy-start.3
  2.0 0.9 %copy-start.1 = (bf16[1,2,256,256]{3,2,1,0:T(8,128)(2,1)S(1)}, bf16[1,2,256,256]{3,2,1,0:T(8,128)(2,1)}, u32[]{:S(2)}) copy-start(bf16[1,2,256,256]{3,2,1,0:T(8,128)(2,1)} %param.7) | copy-start | bytes 786436
  25.4 17.1 %copy-start = (f32[1,256,1024]{2,1,0:T(8,128)S(1)}, f32[1,256,1024]{2,1,0:T(8,128)}, u32[]{:S(2)}) copy-start(f32[1,256,1024]{2,1,0:T(8,128)} %param.10) | copy-start | bytes 3145732
  25.4 17.1 %copy-start.2 = (bf16[1,2,256,256]{3,2,1,0:T(8,128)(2,1)S(1)}, bf16[1,2,256,256]{3,2,1,0:T(8,128)(2,1)}, u32[]{:S(2)}) copy-start(bf16[1,2,256,256]{3,2,1,0:T(8,128)(2,1)} %param.7) | copy-start | bytes 786436
  25.4 17.1 %copy-start.4 = (f32[1,256]{1,0:T(1,128)S(1)}, f32[1,256]{1,0:T(1,128)}, u32[]{:S(2)}) copy-start(f32[1,256]{1,0:T(1,128)} %gain_ref.1) | copy-start | bytes 3076
  56.2 27.4 %copy-start.5 = (f32[1,256,1024]{2,1,0:T(8,128)S(1)}, f32[1,256,1024]{2,1,0:T(8,128)}, u32[]{:S(2)}) copy-start(f32[1,256,1024]{2,1,0:T(8,128)} %param.12) | copy-start | bytes 3145732
  78.7 14.6 %all-to-all-start.4 = ((bf16[16,64,128]{2,1,0:T(8,128)(2,1)}), bf16[16,64,128]{2,1,0:T(8,128)(2,1)S(1)}, u32[]{:S(2)}, u32[]{:S(2)}) async-start(bf16[16,64,128]{2,1,0:T(8,128)(2,1)} %get-tuple-element.15), calls=%async_computation.4 | async-start | bytes 524288 | tf_op jit(solution)/shard_map/all_to_all | solution.py:50

commit v3 on v1

--- a/solution.py
+++ b/solution.py
@@ -41,7 +41,8 @@
 
 
 RING = [3 * r % 8 for r in range(8)]
-Y_PEERS = [y * 2 + core for core in range(2) for y in RING]
+MIXED = [0, 1, 7, 2, 6, 3, 5, 4]
+Y_PEERS = [y * 2 + core for core in range(2) for y in MIXED]
 
 
 def swap(blocks, axis, peers=None):
@@ -173,7 +174,7 @@
 
 
 def on_device(hidden, gain, key_grad, master, moment, second, overflow):
-    block = call(key_kernel, sds((128, 128), bf16), 1, 0, 64 * 1024)(key_grad.reshape(16, K))
+    block = call(key_kernel, sds((128, 128), bf16), 1, 4 * F * TOK * K, 4 * 1024 * 1024)(key_grad.reshape(16, K))
     send, flags = call(
         first_kernel, (sds((NZ, 136, 128), bf16), sds((8, 128))), 2, 3 * F * TOK, F * TOK * 2, (), 1
     )(overflow, hidden[0], block)

time: 94.7 us -> 94 us (level); the launches traced: 92.8 us -> 93.6 us
  waiting for transfers between devices: 3.79 us -> 5.42 us
  blocking collectives: 72.2 us -> 73.8 us
  starting transfers between devices: 5.95 us -> 4.36 us
  local copies, waits for them, and re-layouts: 2.3 us -> 1.35 us
    all_to_all x1, waiting for transfers between devices: 3.79 us -> 5.42 us  [swap(): lax.all_to_all(blocks, axis, split_axis=0, concat_axis=0, tiled=True, axi...]
    all_to_all x1, starting transfers between devices: 5.95 us -> 4.36 us  [swap(): lax.all_to_all(blocks, axis, split_axis=0, concat_axis=0, tiled=True, axi...]
    all_to_all x4, blocking collectives: 72.2 us -> 73.8 us  [swap(): lax.all_to_all(blocks, axis, split_axis=0, concat_axis=0, tiled=True, axi...]
    unnamed x12 -> x10, local copies, waits for them, and re-layouts: 1.72 us -> 0.77 us
where the time goes in v3:
time: 94 us; the launch traced here: 93.6 us
  blocking collectives  73.8 us (79%)
  waiting for transfers between devices  5.42 us (6%)
  starting transfers between devices  4.36 us (5%)
  other arithmetic  4.26 us (5%)
  Pallas kernels  2.97 us (3%)
  between operations  1.38 us (1%)
  local copies, waits for them, and re-layouts  1.35 us (1%)
    all_to_all x4, blocking collectives, swap(): lax.all_to_all(blocks, axis, split_axis=0, concat_axis=0, tiled=True, axi...  73.8 us
    all_to_all x1, waiting for transfers between devices, swap(): lax.all_to_all(blocks, axis, split_axis=0, concat_axis=0, tiled=True, axi...  5.42 us
    all_to_all x1, starting transfers between devices, swap(): lax.all_to_all(blocks, axis, split_axis=0, concat_axis=0, tiled=True, axi...  4.36 us
    broadcast_in_dim x1, other arithmetic, on_device(): return (grad_input[None], (clip[4, 0] * update)[None])  4.26 us
  transfers between devices with their start and end apart: 1, of which 1 were waited for; matrix products, arithmetic and copies ran while one was open for 5% of the time, Pallas kernels for 0%

profile of v3, /device:TPU:1, one launch (start us, length us, event | category | flops | bytes accessed | tf_op | source)
XLA Modules:
  0.0 93.6 jit_solution(6731848459260988948)
XLA Ops:
  0.6 0.0 copy-start.1
  1.3 0.0 copy-start.3
  1.3 0.7 copy-done.3
  2.1 0.0 copy-done.1
  2.1 0.2 shard_map.87
  2.3 20.5 %all_to_all.25.got_ref = bf16[8,136,128]{2,1,0:T(8,128)(2,1)S(1)} all-to-all(bf16[8,136,128]{2,1,0:T(8,128)(2,1)S(1)} %get-tuple-element.11), channel_id=1, replica_groups={{0,12,24,4,16,28,8,20},{1,13,25,5,17,29,9,21},{2,14,26,6,18,30,10,22},{..., dimensions={0} | all-to-all | bytes 557056 | tf_op jit(solution)/shard_map/all_to_all | solution.py:50
  22.8 0.1 shard_map.88
  23.0 0.0 copy-start
  23.0 0.0 copy-start.2
  23.0 15.3 %all_to_all.26.got_ref = bf16[4,1032,128]{2,1,0:T(8,128)(2,1)S(1)} all-to-all(bf16[4,1032,128]{2,1,0:T(8,128)(2,1)S(1)} %shard_map.88), channel_id=1, replica_groups=mesh['y'=8,'core'=2,'z'=8,'x'=4] {'x'}, dimensions={0} | all-to-all | bytes 2113536 | tf_op jit(solution)/shard_map/all_to_all | solution.py:50
  38.3 0.0 copy-done
  38.3 0.0 copy-done.2
  38.3 1.0 %shard_map.89 = (f32[256,1024]{1,0:T(8,128)S(1)}, f32[256,512]{1,0:T(8,128)S(1)}, f32[256,512]{1,0:T(8,128)S(1)}, f32[32,1,640]{2,1,0:T(1,128)S(1)}) custom-call(f32[8,128]{1,0:T(8,128)S(1)} %get-tuple-element.10.flags_ref, bf16[2,256,256]{2,1,0:T(8,128)(2,1)S(1)} %bitcast.23, bf16[4,1032,128]{2,1,0:T(8,128)(2,1)S(1)} %all_to_all.26.got_ref, ...), custom_call_target="tpu_custom_call" | custom-call | flops 536870912 | bytes 4194304 | tf_op jit(solution)/shard_map/pallas_call | solution.py:184
  39.3 16.5 %all_to_all.27.got_ref = f32[32,1,640]{2,1,0:T(1,128)S(1)} all-to-all(f32[32,1,640]{2,1,0:T(1,128)S(1)} %get-tuple-element.14), channel_id=1, replica_groups=mesh['y'=8,'core'=2,'z'=8,'x'=4] {'z','x'}, dimensions={0} | all-to-all | bytes 163840 | tf_op jit(solution)/shard_map/all_to_all | solution.py:50
  55.8 0.1 shard_map.90
  55.9 0.0 copy-start.4
  55.9 21.4 %all_to_all.28.got_ref = bf16[16,72,128]{2,1,0:T(8,128)(2,1)S(1)} all-to-all(bf16[16,72,128]{2,1,0:T(8,128)(2,1)S(1)} %shard_map.90), channel_id=1, replica_groups={{0,64,448,128,384,192,320,256,32,96,480,160,416,224,352,288},{1,65,449,..., dimensions={0} | all-to-all | bytes 589824 | tf_op jit(solution)/shard_map/all_to_all | solution.py:50
  77.4 0.7 shard_map.91
  78.1 4.4 %all-to-all-start.4 = ((bf16[16,64,128]{2,1,0:T(8,128)(2,1)}), bf16[16,64,128]{2,1,0:T(8,128)(2,1)S(1)}, u32[]{:S(2)}, u32[]{:S(2)}) async-start(bf16[16,64,128]{2,1,0:T(8,128)(2,1)} %get-tuple-element.15), calls=%async_computation.4 | async-start | bytes 524288 | tf_op jit(solution)/shard_map/all_to_all | solution.py:50
  82.5 0.6 fusion.7
  83.0 0.0 copy-done.4
  83.0 4.3 %multiply_bitcast_fusion = f32[1,256,1024]{2,1,0:T(8,128)} fusion(f32[1,256,1024]{2,1,0:T(8,128)S(1)} %copy-done.4, f32[256,1024]{1,0:T(8,128)S(1)} %get-tuple-element.17, f32[1,256,1024]{2,1,0:T(8,128)} %param.11, f32[]{:T(128)} %bitcast.6, f32[]{:T(128)} %bitcast.4, f32[1,256,1024]{2,1,0:T(8,128)S(1)} %copy-done), kind=kLoop, calls=%fused_computation.9 | loop fusion | flops 3932160 | bytes 5242888 | tf_op jit(solution)/shard_map/broadcast_in_dim | solution.py:206
  87.3 5.4 %all-to-all-done.4.back_ref = bf16[16,64,128]{2,1,0:T(8,128)(2,1)S(1)} async-done(((bf16[16,64,128]{2,1,0:T(8,128)(2,1)}), bf16[16,64,128]{2,1,0:T(8,128)(2,1)S(1)}, u32[]{:S(2)}, u32[]{:S(2)}) %all-to-all-start.4) | async-done | bytes 262176 | tf_op jit(solution)/shard_map/all_to_all | solution.py:50
  92.7 0.8 shard_map.92
  (1 shorter events, 0.0 us)
Async XLA Ops:
  0.6 1.5 %copy-start.1 = (bf16[1,2,256,256]{3,2,1,0:T(8,128)(2,1)S(1)}, bf16[1,2,256,256]{3,2,1,0:T(8,128)(2,1)}, u32[]{:S(2)}) copy-start(bf16[1,2,256,256]{3,2,1,0:T(8,128)(2,1)} %param.7) | copy-start | bytes 786436
  1.3 0.8 copy-start.3
  23.0 15.4 %copy-start = (f32[1,256,1024]{2,1,0:T(8,128)S(1)}, f32[1,256,1024]{2,1,0:T(8,128)}, u32[]{:S(2)}) copy-start(f32[1,256,1024]{2,1,0:T(8,128)} %param.10) | copy-start | bytes 3145732
  23.0 15.3 %copy-start.2 = (f32[1,256]{1,0:T(1,128)S(1)}, f32[1,256]{1,0:T(1,128)}, u32[]{:S(2)}) copy-start(f32[1,256]{1,0:T(1,128)} %gain_ref.1) | copy-start | bytes 3076
  55.9 27.1 %copy-start.4 = (f32[1,256,1024]{2,1,0:T(8,128)S(1)}, f32[1,256,1024]{2,1,0:T(8,128)}, u32[]{:S(2)}) copy-start(f32[1,256,1024]{2,1,0:T(8,128)} %param.12) | copy-start | bytes 3145732
  78.1 14.6 %all-to-all-start.4 = ((bf16[16,64,128]{2,1,0:T(8,128)(2,1)}), bf16[16,64,128]{2,1,0:T(8,128)(2,1)S(1)}, u32[]{:S(2)}, u32[]{:S(2)}) async-start(bf16[16,64,128]{2,1,0:T(8,128)(2,1)} %get-tuple-element.15), calls=%async_computation.4 | async-start | bytes 524288 | tf_op jit(solution)/shard_map/all_to_all | solution.py:50

commit v4 on v3

--- a/solution.py
+++ b/solution.py
@@ -40,7 +40,6 @@
     return jax.ShapeDtypeStruct(shape, dtype)
 
 
-RING = [3 * r % 8 for r in range(8)]
 MIXED = [0, 1, 7, 2, 6, 3, 5, 4]
 Y_PEERS = [y * 2 + core for core in range(2) for y in MIXED]
 
@@ -94,7 +93,7 @@
         total = total + join_rows(got_ref[z, 128:136, :])
     sums = split_rows(as_row(total))
     for peer in range(NX):
-        for r, z in enumerate(RING):
+        for r, z in enumerate(MIXED):
             send_ref[peer, z * 128 : (z + 1) * 128, :] = got_ref[r, 0:128, :]
         send_ref[peer, 1024:1032, :] = sums[0:8]
 
@@ -178,7 +177,7 @@
     send, flags = call(
         first_kernel, (sds((NZ, 136, 128), bf16), sds((8, 128))), 2, 3 * F * TOK, F * TOK * 2, (), 1
     )(overflow, hidden[0], block)
-    got = swap(send, "z", RING)
+    got = swap(send, "z", MIXED)
     send = call(middle_kernel, sds((NX, 1032, 128), bf16), 1, 0, 1024 * 1024)(got)
     got = swap(send, "x")
     gw, plain, slope, send = call(

time: 94 us -> 93.7 us (level)
  no operation moved by 1% of the time
where the time goes in v4:
time: 93.7 us; the launch traced here: 93.2 us
  blocking collectives  73.5 us (78%)
  waiting for transfers between devices  5.42 us (6%)
  starting transfers between devices  4.36 us (5%)
  other arithmetic  4.26 us (5%)
  Pallas kernels  2.97 us (3%)
  between operations  1.38 us (1%)
  local copies, waits for them, and re-layouts  1.35 us (1%)
    all_to_all x4, blocking collectives, swap(): lax.all_to_all(blocks, axis, split_axis=0, concat_axis=0, tiled=True, axi...  73.5 us
    all_to_all x1, waiting for transfers between devices, swap(): lax.all_to_all(blocks, axis, split_axis=0, concat_axis=0, tiled=True, axi...  5.42 us
    all_to_all x1, starting transfers between devices, swap(): lax.all_to_all(blocks, axis, split_axis=0, concat_axis=0, tiled=True, axi...  4.36 us
    broadcast_in_dim x1, other arithmetic, on_device(): return (grad_input[None], (clip[4, 0] * update)[None])  4.26 us
  transfers between devices with their start and end apart: 1, of which 1 were waited for; matrix products, arithmetic and copies ran while one was open for 5% of the time, Pallas kernels for 0%

profile of v4, /device:TPU:1, one launch (start us, length us, event | category | flops | bytes accessed | tf_op | source)
XLA Modules:
  0.0 93.2 jit_solution(18102585211041895144)
XLA Ops:
  0.6 0.0 copy-start.1
  1.3 0.0 copy-start.3
  1.3 0.7 copy-done.3
  2.1 0.0 copy-done.1
  2.1 0.2 shard_map.87
  2.3 22.1 %all_to_all.25.got_ref = bf16[8,136,128]{2,1,0:T(8,128)(2,1)S(1)} all-to-all(bf16[8,136,128]{2,1,0:T(8,128)(2,1)S(1)} %get-tuple-element.11), channel_id=1, replica_groups={{0,4,28,8,24,12,20,16},{1,5,29,9,25,13,21,17},{2,6,30,10,26,14,22,18},{..., dimensions={0} | all-to-all | bytes 557056 | tf_op jit(solution)/shard_map/all_to_all | solution.py:49
  24.4 0.1 shard_map.88
  24.5 0.0 copy-start
  24.5 0.0 copy-start.2
  24.5 16.8 %all_to_all.26.got_ref = bf16[4,1032,128]{2,1,0:T(8,128)(2,1)S(1)} all-to-all(bf16[4,1032,128]{2,1,0:T(8,128)(2,1)S(1)} %shard_map.88), channel_id=1, replica_groups=mesh['y'=8,'core'=2,'z'=8,'x'=4] {'x'}, dimensions={0} | all-to-all | bytes 2113536 | tf_op jit(solution)/shard_map/all_to_all | solution.py:49
  41.3 0.0 copy-done
  41.3 0.0 copy-done.2
  41.3 1.0 %shard_map.89 = (f32[256,1024]{1,0:T(8,128)S(1)}, f32[256,512]{1,0:T(8,128)S(1)}, f32[256,512]{1,0:T(8,128)S(1)}, f32[32,1,640]{2,1,0:T(1,128)S(1)}) custom-call(f32[8,128]{1,0:T(8,128)S(1)} %get-tuple-element.10.flags_ref, bf16[2,256,256]{2,1,0:T(8,128)(2,1)S(1)} %bitcast.23, bf16[4,1032,128]{2,1,0:T(8,128)(2,1)S(1)} %all_to_all.26.got_ref, ...), custom_call_target="tpu_custom_call" | custom-call | flops 536870912 | bytes 4194304 | tf_op jit(solution)/shard_map/pallas_call | solution.py:183
  42.3 12.9 %all_to_all.27.got_ref = f32[32,1,640]{2,1,0:T(1,128)S(1)} all-to-all(f32[32,1,640]{2,1,0:T(1,128)S(1)} %get-tuple-element.14), channel_id=1, replica_groups=mesh['y'=8,'core'=2,'z'=8,'x'=4] {'z','x'}, dimensions={0} | all-to-all | bytes 163840 | tf_op jit(solution)/shard_map/all_to_all | solution.py:49
  55.2 0.1 shard_map.90
  55.3 0.0 copy-start.4
  55.3 21.8 %all_to_all.28.got_ref = bf16[16,72,128]{2,1,0:T(8,128)(2,1)S(1)} all-to-all(bf16[16,72,128]{2,1,0:T(8,128)(2,1)S(1)} %shard_map.90), channel_id=1, replica_groups={{0,64,448,128,384,192,320,256,32,96,480,160,416,224,352,288},{1,65,449,..., dimensions={0} | all-to-all | bytes 589824 | tf_op jit(solution)/shard_map/all_to_all | solution.py:49
  77.0 0.7 shard_map.91
  77.8 4.4 %all-to-all-start.4 = ((bf16[16,64,128]{2,1,0:T(8,128)(2,1)}), bf16[16,64,128]{2,1,0:T(8,128)(2,1)S(1)}, u32[]{:S(2)}, u32[]{:S(2)}) async-start(bf16[16,64,128]{2,1,0:T(8,128)(2,1)} %get-tuple-element.15), calls=%async_computation.4 | async-start | bytes 524288 | tf_op jit(solution)/shard_map/all_to_all | solution.py:49
  82.1 0.6 fusion.7
  82.7 0.0 copy-done.4
  82.7 4.3 %multiply_bitcast_fusion = f32[1,256,1024]{2,1,0:T(8,128)} fusion(f32[1,256,1024]{2,1,0:T(8,128)S(1)} %copy-done.4, f32[256,1024]{1,0:T(8,128)S(1)} %get-tuple-element.17, f32[1,256,1024]{2,1,0:T(8,128)} %param.11, f32[]{:T(128)} %bitcast.6, f32[]{:T(128)} %bitcast.4, f32[1,256,1024]{2,1,0:T(8,128)S(1)} %copy-done), kind=kLoop, calls=%fused_computation.9 | loop fusion | flops 3932160 | bytes 5242888 | tf_op jit(solution)/shard_map/broadcast_in_dim | solution.py:205
  87.0 5.4 %all-to-all-done.4.back_ref = bf16[16,64,128]{2,1,0:T(8,128)(2,1)S(1)} async-done(((bf16[16,64,128]{2,1,0:T(8,128)(2,1)}), bf16[16,64,128]{2,1,0:T(8,128)(2,1)S(1)}, u32[]{:S(2)}, u32[]{:S(2)}) %all-to-all-start.4) | async-done | bytes 262176 | tf_op jit(solution)/shard_map/all_to_all | solution.py:49
  92.4 0.8 shard_map.92
  (1 shorter events, 0.0 us)
Async XLA Ops:
  0.6 1.5 %copy-start.1 = (bf16[1,2,256,256]{3,2,1,0:T(8,128)(2,1)S(1)}, bf16[1,2,256,256]{3,2,1,0:T(8,128)(2,1)}, u32[]{:S(2)}) copy-start(bf16[1,2,256,256]{3,2,1,0:T(8,128)(2,1)} %param.7) | copy-start | bytes 786436
  1.3 0.8 copy-start.3
  24.5 16.8 %copy-start = (f32[1,256,1024]{2,1,0:T(8,128)S(1)}, f32[1,256,1024]{2,1,0:T(8,128)}, u32[]{:S(2)}) copy-start(f32[1,256,1024]{2,1,0:T(8,128)} %param.10) | copy-start | bytes 3145732
  24.5 16.8 %copy-start.2 = (f32[1,256]{1,0:T(1,128)S(1)}, f32[1,256]{1,0:T(1,128)}, u32[]{:S(2)}) copy-start(f32[1,256]{1,0:T(1,128)} %gain_ref.1) | copy-start | bytes 3076
  55.3 27.4 %copy-start.4 = (f32[1,256,1024]{2,1,0:T(8,128)S(1)}, f32[1,256,1024]{2,1,0:T(8,128)}, u32[]{:S(2)}) copy-start(f32[1,256,1024]{2,1,0:T(8,128)} %param.12) | copy-start | bytes 3145732
  77.8 14.6 %all-to-all-start.4 = ((bf16[16,64,128]{2,1,0:T(8,128)(2,1)}), bf16[16,64,128]{2,1,0:T(8,128)(2,1)S(1)}, u32[]{:S(2)}, u32[]{:S(2)}) async-start(bf16[16,64,128]{2,1,0:T(8,128)(2,1)} %get-tuple-element.15), calls=%async_computation.4 | async-start | bytes 524288 | tf_op jit(solution)/shard_map/all_to_all | solution.py:49

commit v5 on v4

--- a/solution.py
+++ b/solution.py
@@ -80,7 +80,7 @@
     sums = split_rows(jnp.sum(xt * xt, axis=0, keepdims=True))
     for peer in range(NZ):
         send_ref[peer, 0:128, :] = block_ref[...]
-        send_ref[peer, 128:136, :] = sums[0:8]
+        send_ref[peer, 128:144, :] = sums
     flag = flag_ref[0]
     factor = jnp.where(flag == 0, 1.0, jnp.where(flag == 1, 0.5, 0.0)).astype(f32)
     keep = jnp.where(flag == 2, 0.0, 1.0).astype(f32)
@@ -90,12 +90,12 @@
 def middle_kernel(got_ref, send_ref):
     total = jnp.zeros((4, 128), f32)
     for z in range(NZ):
-        total = total + join_rows(got_ref[z, 128:136, :])
+        total = total + join_rows(got_ref[z, 128:144, :])
     sums = split_rows(as_row(total))
     for peer in range(NX):
         for r, z in enumerate(MIXED):
             send_ref[peer, z * 128 : (z + 1) * 128, :] = got_ref[r, 0:128, :]
-        send_ref[peer, 1024:1032, :] = sums[0:8]
+        send_ref[peer, 1024:1040, :] = sums
 
 
 def main_kernel(
@@ -110,7 +110,7 @@
                 ]
     total = jnp.zeros((4, 128), f32)
     for x in range(NX):
-        total = total + join_rows(got_ref[x, 1024:1032, :])
+        total = total + join_rows(got_ref[x, 1024:1040, :])
     inv = lax.rsqrt(as_row(total) * (1.0 / D) + 1e-05)
     col = jnp.broadcast_to(gain_ref[...], (8, F)).T[:, 0:1]
     xt = features_first(x_ref)
@@ -148,7 +148,7 @@
     for j in range(SEC):
         for q in range(4):
             send_ref[j, q * 16 : (q + 1) * 16, :] = sent[j * 16 : (j + 1) * 16, q * 128 : (q + 1) * 128]
-        send_ref[j, 64:72, :] = layer_sq[0:8]
+        send_ref[j, 64:80, :] = layer_sq
 
 
 def suffix_kernel(got_ref, flags_ref, back_ref, clip_ref):
@@ -158,7 +158,7 @@
         s = Y_PEERS.index(layer)
         running = running + got_ref[s, 0:64, :].astype(f32)
         back_ref[s] = running.astype(bf16)
-        norm = norm + join_rows(got_ref[s, 64:72, :])
+        norm = norm + join_rows(got_ref[s, 64:80, :])
     clip = jnp.minimum(1.0, clip_norm / (jnp.sqrt(norm) + 1e-06))
     clip_ref[...] = jnp.concatenate([clip, flags_ref[4:8, :]], axis=0)
 
@@ -175,10 +175,10 @@
 def on_device(hidden, gain, key_grad, master, moment, second, overflow):
     block = call(key_kernel, sds((128, 128), bf16), 1, 4 * F * TOK * K, 4 * 1024 * 1024)(key_grad.reshape(16, K))
     send, flags = call(
-        first_kernel, (sds((NZ, 136, 128), bf16), sds((8, 128))), 2, 3 * F * TOK, F * TOK * 2, (), 1
+        first_kernel, (sds((NZ, 144, 128), bf16), sds((8, 128))), 2, 3 * F * TOK, F * TOK * 2, (), 1
     )(overflow, hidden[0], block)
     got = swap(send, "z", MIXED)
-    send = call(middle_kernel, sds((NX, 1032, 128), bf16), 1, 0, 1024 * 1024)(got)
+    send = call(middle_kernel, sds((NX, 1040, 128), bf16), 1, 0, 1024 * 1024)(got)
     got = swap(send, "x")
     gw, plain, slope, send = call(
         main_kernel,
@@ -189,7 +189,7 @@
         [pltpu.VMEM((TOK, K), bf16), pltpu.VMEM((F, TOK), bf16)],
     )(flags, hidden[0], got, gain, master[0])
     got = swap(send, ("z", "x"))
-    send = call(branch_kernel, sds((SEC, 72, 128), bf16), 3, 3 * F * TOK, 1024 * 1024)(plain, slope, got)
+    send = call(branch_kernel, sds((SEC, 80, 128), bf16), 3, 3 * F * TOK, 1024 * 1024)(plain, slope, got)
     got = swap(send, ("y", "core"), Y_PEERS)
     back, clip = call(
         suffix_kernel, (sds((SEC, 64, 128), bf16), sds((8, 128))), 2, 4 * F * TOK, 1024 * 1024

time: 93.7 us -> 94.9 us (1.013)
  blocking collectives: 73.5 us -> 74.7 us
    all_to_all x4, blocking collectives: 73.5 us -> 74.7 us  [swap(): lax.all_to_all(blocks, axis, split_axis=0, concat_axis=0, tiled=True, axi...]
where the time goes in v5:
time: 94.9 us; the launch traced here: 94.4 us
  blocking collectives  74.7 us (79%)
  waiting for transfers between devices  5.42 us (6%)
  starting transfers between devices  4.34 us (5%)
  other arithmetic  4.26 us (4%)
  Pallas kernels  2.98 us (3%)
  between operations  1.38 us (1%)
  local copies, waits for them, and re-layouts  1.35 us (1%)
    all_to_all x4, blocking collectives, swap(): lax.all_to_all(blocks, axis, split_axis=0, concat_axis=0, tiled=True, axi...  74.7 us
    all_to_all x1, waiting for transfers between devices, swap(): lax.all_to_all(blocks, axis, split_axis=0, concat_axis=0, tiled=True, axi...  5.42 us
    all_to_all x1, starting transfers between devices, swap(): lax.all_to_all(blocks, axis, split_axis=0, concat_axis=0, tiled=True, axi...  4.34 us
    broadcast_in_dim x1, other arithmetic, on_device(): return (grad_input[None], (clip[4, 0] * update)[None])  4.26 us
  transfers between devices with their start and end apart: 1, of which 1 were waited for; matrix products, arithmetic and copies ran while one was open for 5% of the time, Pallas kernels for 0%

profile of v5, /device:TPU:1, one launch (start us, length us, event | category | flops | bytes accessed | tf_op | source)
XLA Modules:
  0.0 94.4 jit_solution(6342497331194935378)
XLA Ops:
  0.6 0.0 copy-start.1
  1.3 0.0 copy-start.3
  1.3 0.7 copy-done.3
  2.1 0.0 copy-done.1
  2.1 0.2 shard_map.87
  2.3 22.4 %all_to_all.25.got_ref = bf16[8,144,128]{2,1,0:T(8,128)(2,1)S(1)} all-to-all(bf16[8,144,128]{2,1,0:T(8,128)(2,1)S(1)} %get-tuple-element.11), channel_id=1, replica_groups={{0,4,28,8,24,12,20,16},{1,5,29,9,25,13,21,17},{2,6,30,10,26,14,22,18},{..., dimensions={0} | all-to-all | bytes 589824 | tf_op jit(solution)/shard_map/all_to_all | solution.py:49
  24.7 0.1 shard_map.88
  24.8 0.0 copy-start
  24.8 0.0 copy-start.2
  24.8 16.9 %all_to_all.26.got_ref = bf16[4,1040,128]{2,1,0:T(8,128)(2,1)S(1)} all-to-all(bf16[4,1040,128]{2,1,0:T(8,128)(2,1)S(1)} %shard_map.88), channel_id=1, replica_groups=mesh['y'=8,'core'=2,'z'=8,'x'=4] {'x'}, dimensions={0} | all-to-all | bytes 2129920 | tf_op jit(solution)/shard_map/all_to_all | solution.py:49
  41.7 0.0 copy-done
  41.7 0.0 copy-done.2
  41.7 1.0 %shard_map.89 = (f32[256,1024]{1,0:T(8,128)S(1)}, f32[256,512]{1,0:T(8,128)S(1)}, f32[256,512]{1,0:T(8,128)S(1)}, f32[32,1,640]{2,1,0:T(1,128)S(1)}) custom-call(f32[8,128]{1,0:T(8,128)S(1)} %get-tuple-element.10.flags_ref, bf16[2,256,256]{2,1,0:T(8,128)(2,1)S(1)} %bitcast.23, bf16[4,1040,128]{2,1,0:T(8,128)(2,1)S(1)} %all_to_all.26.got_ref, ...), custom_call_target="tpu_custom_call" | custom-call | flops 536870912 | bytes 4194304 | tf_op jit(solution)/shard_map/pallas_call | solution.py:183
  42.7 12.9 %all_to_all.27.got_ref = f32[32,1,640]{2,1,0:T(1,128)S(1)} all-to-all(f32[32,1,640]{2,1,0:T(1,128)S(1)} %get-tuple-element.14), channel_id=1, replica_groups=mesh['y'=8,'core'=2,'z'=8,'x'=4] {'z','x'}, dimensions={0} | all-to-all | bytes 163840 | tf_op jit(solution)/shard_map/all_to_all | solution.py:49
  55.7 0.1 shard_map.90
  55.7 0.0 copy-start.4
  55.8 22.5 %all_to_all.28.got_ref = bf16[16,80,128]{2,1,0:T(8,128)(2,1)S(1)} all-to-all(bf16[16,80,128]{2,1,0:T(8,128)(2,1)S(1)} %shard_map.90), channel_id=1, replica_groups={{0,64,448,128,384,192,320,256,32,96,480,160,416,224,352,288},{1,65,449,..., dimensions={0} | all-to-all | bytes 655360 | tf_op jit(solution)/shard_map/all_to_all | solution.py:49
  78.2 0.7 shard_map.91
  79.0 4.3 %all-to-all-start.4 = ((bf16[16,64,128]{2,1,0:T(8,128)(2,1)}), bf16[16,64,128]{2,1,0:T(8,128)(2,1)S(1)}, u32[]{:S(2)}, u32[]{:S(2)}) async-start(bf16[16,64,128]{2,1,0:T(8,128)(2,1)} %get-tuple-element.15), calls=%async_computation.4 | async-start | bytes 524288 | tf_op jit(solution)/shard_map/all_to_all | solution.py:49
  83.3 0.6 fusion.7
  83.9 0.0 copy-done.4
  83.9 4.3 %multiply_bitcast_fusion = f32[1,256,1024]{2,1,0:T(8,128)} fusion(f32[1,256,1024]{2,1,0:T(8,128)S(1)} %copy-done.4, f32[256,1024]{1,0:T(8,128)S(1)} %get-tuple-element.17, f32[1,256,1024]{2,1,0:T(8,128)} %param.11, f32[]{:T(128)} %bitcast.6, f32[]{:T(128)} %bitcast.4, f32[1,256,1024]{2,1,0:T(8,128)S(1)} %copy-done), kind=kLoop, calls=%fused_computation.9 | loop fusion | flops 3932160 | bytes 5242888 | tf_op jit(solution)/shard_map/broadcast_in_dim | solution.py:205
  88.2 5.4 %all-to-all-done.4.back_ref = bf16[16,64,128]{2,1,0:T(8,128)(2,1)S(1)} async-done(((bf16[16,64,128]{2,1,0:T(8,128)(2,1)}), bf16[16,64,128]{2,1,0:T(8,128)(2,1)S(1)}, u32[]{:S(2)}, u32[]{:S(2)}) %all-to-all-start.4) | async-done | bytes 262176 | tf_op jit(solution)/shard_map/all_to_all | solution.py:49
  93.6 0.8 shard_map.92
  (1 shorter events, 0.0 us)
Async XLA Ops:
  0.6 1.5 %copy-start.1 = (bf16[1,2,256,256]{3,2,1,0:T(8,128)(2,1)S(1)}, bf16[1,2,256,256]{3,2,1,0:T(8,128)(2,1)}, u32[]{:S(2)}) copy-start(bf16[1,2,256,256]{3,2,1,0:T(8,128)(2,1)} %param.7) | copy-start | bytes 786436
  1.3 0.8 copy-start.3
  24.8 16.9 %copy-start = (f32[1,256,1024]{2,1,0:T(8,128)S(1)}, f32[1,256,1024]{2,1,0:T(8,128)}, u32[]{:S(2)}) copy-start(f32[1,256,1024]{2,1,0:T(8,128)} %param.10) | copy-start | bytes 3145732
  24.8 16.9 %copy-start.2 = (f32[1,256]{1,0:T(1,128)S(1)}, f32[1,256]{1,0:T(1,128)}, u32[]{:S(2)}) copy-start(f32[1,256]{1,0:T(1,128)} %gain_ref.1) | copy-start | bytes 3076
  55.7 28.2 %copy-start.4 = (f32[1,256,1024]{2,1,0:T(8,128)S(1)}, f32[1,256,1024]{2,1,0:T(8,128)}, u32[]{:S(2)}) copy-start(f32[1,256,1024]{2,1,0:T(8,128)} %param.12) | copy-start | bytes 3145732
  79.0 14.6 %all-to-all-start.4 = ((bf16[16,64,128]{2,1,0:T(8,128)(2,1)}), bf16[16,64,128]{2,1,0:T(8,128)(2,1)S(1)}, u32[]{:S(2)}, u32[]{:S(2)}) async-start(bf16[16,64,128]{2,1,0:T(8,128)(2,1)} %get-tuple-element.15), calls=%async_computation.4 | async-start | bytes 524288 | tf_op jit(solution)/shard_map/all_to_all | solution.py:49
